TPU v7x, 128 devices: a whole 4x4x4 slice. The times are simulated.
128 devices in a mesh: dp: 32 (over x, y, z_lo), tensor: 4 (over z_hi, core).
Axes of the slice: x: 4, y: 4, z: 4 (z_hi: 2, z_lo: 2; z = z_hi * 2 + z_lo), core: 2. Of those that a mesh axis runs over, the one named last changes fastest.
Arguments:
- activations: bfloat16 [1024, 128, 2048], P('dp', None, 'tensor'), may hold values from -6 to 6
- out_grads: bfloat16 [1024, 128, 8192], P('dp', None, 'tensor'), may hold values from -6 to 6
- lengths: int32 [1024], P('dp'), may hold values from 1 to 128
- proj_in: bfloat16 [2048, 64], P('tensor'), may hold values from -0.125 to 0.125
- proj_out: bfloat16 [8192, 64], P('tensor'), may hold values from -0.0625 to 0.0625
- query_grads: bfloat16 [2048, 4096], P('dp', 'tensor'), may hold values from -400 to 400, as said below
Outputs:
- scores: float32 [1024, 2048], P('dp')
Inputs may be any that keep to these rules, and one draw needn't show every extreme that they name: `query_grads`: entries have different typical sizes from column to column and from row to row.
All inputs are finite; a program needn't handle non-finite values.
Results may differ from a plain program's by a relative error of at most 0.005.
Values may be sent and summed in bfloat16 or wider, within the bound.
A program may use at most 64 MiB of HBM per device.

v0:
```python
import jax
import jax.numpy as jnp
from jax import lax
from jax.sharding import PartitionSpec as P

eps = 1e-06


def shifted(array, axis, by):
    devices = lax.axis_size(axis)
    return lax.ppermute(array, axis, [(i, (i + by) % devices) for i in range(devices)])


def on_device(activations, out_grads, lengths, proj_in, proj_out, query_grads):
    train_rows, seq_len, in_width = activations.shape
    rank_size = proj_in.shape[1]
    tensor_count = lax.axis_size("tensor")
    slice_width = rank_size // tensor_count
    cycle_size = lax.axis_size("dp")
    cycle_place = lax.axis_index("dp")
    query_rows = query_grads.shape[0]
    part_in = jnp.dot(
        activations.reshape(train_rows * seq_len, in_width),
        proj_in,
        preferred_element_type=jnp.float32,
    )
    part_out = jnp.dot(
        out_grads.reshape(train_rows * seq_len, out_grads.shape[2]),
        proj_out,
        preferred_element_type=jnp.float32,
    )
    out_own = lax.psum_scatter(part_out, "tensor", scatter_dimension=1, tiled=True)
    in_full = lax.psum(part_in, "tensor")
    valid_mask = (
        lax.broadcasted_iota(jnp.int32, (train_rows, seq_len), 1) < lengths[:, None]
    ).astype(jnp.float32)
    out_low = (
        (out_own * valid_mask.reshape(-1, 1))
        .astype(jnp.bfloat16)
        .reshape(train_rows, seq_len, slice_width)
    )
    in_low = in_full.astype(jnp.bfloat16).reshape(train_rows, seq_len, rank_size)
    train_grads = jnp.einsum("tlr,tls->trs", out_low, in_low, preferred_element_type=jnp.float32)
    train_grads = train_grads.astype(jnp.bfloat16).reshape(train_rows, slice_width * rank_size)
    train_sq = jnp.sum(jnp.square(train_grads.astype(jnp.float32)), axis=1)
    query_sq = jnp.sum(jnp.square(query_grads.astype(jnp.float32)), axis=1)
    train_sq, query_sq = lax.psum((train_sq, query_sq), "tensor")
    train_scale = rank_size * lax.rsqrt(train_sq + eps)
    query_scale = lax.rsqrt(query_sq + eps)

    def inner(left, right):
        return lax.dot_general(
            left, right, (((1,), (1,)), ((), ())), preferred_element_type=jnp.float32
        )

    def place_query(buffer, block, owner):
        return lax.dynamic_update_slice_in_dim(
            buffer, inner(train_grads, block), owner * query_rows, 1
        )

    def query_turn(turn_index, carry):
        buffer, block = carry
        buffer = place_query(buffer, block, (cycle_place - turn_index) % cycle_size)
        block = shifted(block, "dp", 1)
        return (buffer, block)

    all_scales = lax.all_gather(query_scale, "dp", axis=0, tiled=True)
    buffer = jnp.zeros((train_rows, cycle_size * query_rows), jnp.float32)
    buffer, block = lax.fori_loop(0, cycle_size - 1, query_turn, (buffer, query_grads))
    buffer = place_query(buffer, block, (cycle_place - (cycle_size - 1)) % cycle_size)
    partial_scores = buffer * all_scales[None, :]
    totals = lax.psum(partial_scores, "tensor")
    return totals * train_scale[:, None]


def solution(mesh):
    placed = (
        P("dp", None, "tensor"),
        P("dp", None, "tensor"),
        P("dp"),
        P("tensor", None),
        P("tensor", None),
        P("dp", "tensor"),
    )
    return jax.shard_map(
        on_device, mesh=mesh, in_specs=placed, out_specs=P("dp", None), check_vma=False
    )
```

profile of v0, /device:TPU:1, one launch (start us, length us, event | category | flops | bytes accessed | tf_op | source)
XLA Modules:
  0.0 490.5 jit_solution(13883147877789436829)
XLA Ops:
  7.6 11.9 %fusion.6 = f32[4096,64]{0,1:T(8,128)} fusion(bf16[4096,2048]{1,0:T(8,128)(2,1)} %bitcast.37, bf16[2048,64]{0,1:T(8,128)(2,1)S(1)} %copy-done), kind=kOutput, calls=%fused_computation.17 | convolution fusion | flops 1073741824 | bytes 18087936 | tf_op jit(solution)/shard_map/dot_general | solution.py:27
  24.6 37.8 %all-reduce.6 = bf16[4096,64]{0,1:T(8,128)(2,1)S(1)} all-reduce(f32[4096,64]{0,1:T(8,128)S(1)} %fusion.7), channel_id=1, replica_groups=mesh['dp'=32,'tensor'=4] {'tensor'}, use_global_device_ids=true, to_apply=%region_1.0 | all-reduce | flops 262144 | bytes 1572864 | tf_op jit(solution)/shard_map/psum | solution.py:33
  64.1 259.7 %while.17 = (s32[]{:T(128)}, f32[32,2048]{1,0:T(8,128)S(1)}, bf16[64,1024]{1,0:T(8,128)(2,1)S(1)}, bf16[32,1024]{1,0:T(8,128)(2,1)S(1)}, s32[]{:T(128)}, /*index...) while((s32[]{:T(128)}, f32[32,2048]{1,0:T(8,128)S(1)}, ...), condition=%wide.region_3.0_spmd, body=%wide.region_2.0_spmd.sunk | while | flops 4194322 | bytes 1007936 | solution.py:69
  65.5 7.8 %collective-permute-done = bf16[64,1024]{1,0:T(8,128)(2,1)S(1)} collective-permute-done((bf16[64,1024]{1,0:T(8,128)(2,1)S(1)}, bf16[64,1024]{1,0:T(8,128)(2,1)S(1)}, u32[]{:S(2)}, u32[]{:S(2)}) %collective-permute-start) | collective-permute-done | bytes 131104 | tf_op jit(solution)/shard_map/while/body/eval_jaxpr/ppermute | solution.py:11
  81.9 7.6 %collective-permute-done = bf16[64,1024]{1,0:T(8,128)(2,1)S(1)} collective-permute-done((bf16[64,1024]{1,0:T(8,128)(2,1)S(1)}, bf16[64,1024]{1,0:T(8,128)(2,1)S(1)}, u32[]{:S(2)}, u32[]{:S(2)}) %collective-permute-start) | collective-permute-done | bytes 131104 | tf_op jit(solution)/shard_map/while/body/eval_jaxpr/ppermute | solution.py:11
  98.3 7.5 %collective-permute-done = bf16[64,1024]{1,0:T(8,128)(2,1)S(1)} collective-permute-done((bf16[64,1024]{1,0:T(8,128)(2,1)S(1)}, bf16[64,1024]{1,0:T(8,128)(2,1)S(1)}, u32[]{:S(2)}, u32[]{:S(2)}) %collective-permute-start) | collective-permute-done | bytes 131104 | tf_op jit(solution)/shard_map/while/body/eval_jaxpr/ppermute | solution.py:11
  114.5 7.5 %collective-permute-done = bf16[64,1024]{1,0:T(8,128)(2,1)S(1)} collective-permute-done((bf16[64,1024]{1,0:T(8,128)(2,1)S(1)}, bf16[64,1024]{1,0:T(8,128)(2,1)S(1)}, u32[]{:S(2)}, u32[]{:S(2)}) %collective-permute-start) | collective-permute-done | bytes 131104 | tf_op jit(solution)/shard_map/while/body/eval_jaxpr/ppermute | solution.py:11
  122.7 7.9 %collective-permute-done = bf16[64,1024]{1,0:T(8,128)(2,1)S(1)} collective-permute-done((bf16[64,1024]{1,0:T(8,128)(2,1)S(1)}, bf16[64,1024]{1,0:T(8,128)(2,1)S(1)}, u32[]{:S(2)}, u32[]{:S(2)}) %collective-permute-start) | collective-permute-done | bytes 131104 | tf_op jit(solution)/shard_map/while/body/eval_jaxpr/ppermute | solution.py:11
  131.2 9.0 %collective-permute-done = bf16[64,1024]{1,0:T(8,128)(2,1)S(1)} collective-permute-done((bf16[64,1024]{1,0:T(8,128)(2,1)S(1)}, bf16[64,1024]{1,0:T(8,128)(2,1)S(1)}, u32[]{:S(2)}, u32[]{:S(2)}) %collective-permute-start) | collective-permute-done | bytes 131104 | tf_op jit(solution)/shard_map/while/body/eval_jaxpr/ppermute | solution.py:11
  140.9 8.0 %collective-permute-done = bf16[64,1024]{1,0:T(8,128)(2,1)S(1)} collective-permute-done((bf16[64,1024]{1,0:T(8,128)(2,1)S(1)}, bf16[64,1024]{1,0:T(8,128)(2,1)S(1)}, u32[]{:S(2)}, u32[]{:S(2)}) %collective-permute-start) | collective-permute-done | bytes 131104 | tf_op jit(solution)/shard_map/while/body/eval_jaxpr/ppermute | solution.py:11
  149.5 7.5 %collective-permute-done = bf16[64,1024]{1,0:T(8,128)(2,1)S(1)} collective-permute-done((bf16[64,1024]{1,0:T(8,128)(2,1)S(1)}, bf16[64,1024]{1,0:T(8,128)(2,1)S(1)}, u32[]{:S(2)}, u32[]{:S(2)}) %collective-permute-start) | collective-permute-done | bytes 131104 | tf_op jit(solution)/shard_map/while/body/eval_jaxpr/ppermute | solution.py:11
  165.8 7.5 %collective-permute-done = bf16[64,1024]{1,0:T(8,128)(2,1)S(1)} collective-permute-done((bf16[64,1024]{1,0:T(8,128)(2,1)S(1)}, bf16[64,1024]{1,0:T(8,128)(2,1)S(1)}, u32[]{:S(2)}, u32[]{:S(2)}) %collective-permute-start) | collective-permute-done | bytes 131104 | tf_op jit(solution)/shard_map/while/body/eval_jaxpr/ppermute | solution.py:11
  182.0 7.5 %collective-permute-done = bf16[64,1024]{1,0:T(8,128)(2,1)S(1)} collective-permute-done((bf16[64,1024]{1,0:T(8,128)(2,1)S(1)}, bf16[64,1024]{1,0:T(8,128)(2,1)S(1)}, u32[]{:S(2)}, u32[]{:S(2)}) %collective-permute-start) | collective-permute-done | bytes 131104 | tf_op jit(solution)/shard_map/while/body/eval_jaxpr/ppermute | solution.py:11
  198.2 8.5 %collective-permute-done = bf16[64,1024]{1,0:T(8,128)(2,1)S(1)} collective-permute-done((bf16[64,1024]{1,0:T(8,128)(2,1)S(1)}, bf16[64,1024]{1,0:T(8,128)(2,1)S(1)}, u32[]{:S(2)}, u32[]{:S(2)}) %collective-permute-start) | collective-permute-done | bytes 131104 | tf_op jit(solution)/shard_map/while/body/eval_jaxpr/ppermute | solution.py:11
  207.5 8.3 %collective-permute-done = bf16[64,1024]{1,0:T(8,128)(2,1)S(1)} collective-permute-done((bf16[64,1024]{1,0:T(8,128)(2,1)S(1)}, bf16[64,1024]{1,0:T(8,128)(2,1)S(1)}, u32[]{:S(2)}, u32[]{:S(2)}) %collective-permute-start) | collective-permute-done | bytes 131104 | tf_op jit(solution)/shard_map/while/body/eval_jaxpr/ppermute | solution.py:11
  216.4 7.5 %collective-permute-done = bf16[64,1024]{1,0:T(8,128)(2,1)S(1)} collective-permute-done((bf16[64,1024]{1,0:T(8,128)(2,1)S(1)}, bf16[64,1024]{1,0:T(8,128)(2,1)S(1)}, u32[]{:S(2)}, u32[]{:S(2)}) %collective-permute-start) | collective-permute-done | bytes 131104 | tf_op jit(solution)/shard_map/while/body/eval_jaxpr/ppermute | solution.py:11
  232.6 7.5 %collective-permute-done = bf16[64,1024]{1,0:T(8,128)(2,1)S(1)} collective-permute-done((bf16[64,1024]{1,0:T(8,128)(2,1)S(1)}, bf16[64,1024]{1,0:T(8,128)(2,1)S(1)}, u32[]{:S(2)}, u32[]{:S(2)}) %collective-permute-start) | collective-permute-done | bytes 131104 | tf_op jit(solution)/shard_map/while/body/eval_jaxpr/ppermute | solution.py:11
  248.9 7.5 %collective-permute-done = bf16[64,1024]{1,0:T(8,128)(2,1)S(1)} collective-permute-done((bf16[64,1024]{1,0:T(8,128)(2,1)S(1)}, bf16[64,1024]{1,0:T(8,128)(2,1)S(1)}, u32[]{:S(2)}, u32[]{:S(2)}) %collective-permute-start) | collective-permute-done | bytes 131104 | tf_op jit(solution)/shard_map/while/body/eval_jaxpr/ppermute | solution.py:11
  265.1 8.2 %collective-permute-done = bf16[64,1024]{1,0:T(8,128)(2,1)S(1)} collective-permute-done((bf16[64,1024]{1,0:T(8,128)(2,1)S(1)}, bf16[64,1024]{1,0:T(8,128)(2,1)S(1)}, u32[]{:S(2)}, u32[]{:S(2)}) %collective-permute-start) | collective-permute-done | bytes 131104 | tf_op jit(solution)/shard_map/while/body/eval_jaxpr/ppermute | solution.py:11
  274.0 8.7 %collective-permute-done = bf16[64,1024]{1,0:T(8,128)(2,1)S(1)} collective-permute-done((bf16[64,1024]{1,0:T(8,128)(2,1)S(1)}, bf16[64,1024]{1,0:T(8,128)(2,1)S(1)}, u32[]{:S(2)}, u32[]{:S(2)}) %collective-permute-start) | collective-permute-done | bytes 131104 | tf_op jit(solution)/shard_map/while/body/eval_jaxpr/ppermute | solution.py:11
  283.3 8.0 %collective-permute-done = bf16[64,1024]{1,0:T(8,128)(2,1)S(1)} collective-permute-done((bf16[64,1024]{1,0:T(8,128)(2,1)S(1)}, bf16[64,1024]{1,0:T(8,128)(2,1)S(1)}, u32[]{:S(2)}, u32[]{:S(2)}) %collective-permute-start) | collective-permute-done | bytes 131104 | tf_op jit(solution)/shard_map/while/body/eval_jaxpr/ppermute | solution.py:11
  323.9 40.7 %all-reduce.1 = (f32[64]{0:T(128)S(1)}, f32[32]{0:T(128)S(1)}) all-reduce(f32[64]{0:T(128)S(1)} %multiply_reduce_fusion.1, f32[32]{0:T(128)S(1)} %get-tuple-element.153), channel_id=1, replica_groups=mesh['dp'=32,'tensor'=4] {'tensor'}, use_global_device_ids=true, to_apply=%region_5.0 | all-reduce | flops 96 | bytes 768 | tf_op jit(solution)/shard_map/psum | solution.py:47
  364.7 64.3 %all-reduce = f32[2048]{0:T(1024)S(1)} all-reduce(f32[2048]{0:T(1024)S(1)} %rsqrt_dynamic-update-slice_fusion), channel_id=1, replica_groups=mesh['dp'=32,'tensor'=4] {'dp'}, use_global_device_ids=true, to_apply=%add | all-reduce | flops 2048 | bytes 16384
  430.3 51.6 %all-reduce.5.cloned.1.call-done = f32[32,2048]{1,0:T(8,128)} async-done(((f32[32,2048]{1,0:T(8,128)}), f32[32,2048]{1,0:T(8,128)}) %all-reduce.5.cloned.1.call-update) | async-done | bytes 262160 | tf_op jit(solution)/shard_map/psum | solution.py:72
  (165 shorter events, 126.3 us)
Async XLA Ops:
  6.5 55.9 %reduce-scatter.2.cloned.1.call-start = ((), (), s32[]{:S(2)}) async-start(), calls=%async_computation.1 | async-start | bytes 1310720 | tf_op jit(solution)/shard_map/reduce_scatter | solution.py:32
  19.5 462.4 %all-reduce.5.cloned.1.call-start = ((), (), s32[]{:S(2)}) async-start(), calls=%async_computation.2 | async-start | bytes 524288 | tf_op jit(solution)/shard_map/psum | solution.py:72
  64.1 9.2 %collective-permute-start = (bf16[64,1024]{1,0:T(8,128)(2,1)S(1)}, bf16[64,1024]{1,0:T(8,128)(2,1)S(1)}, u32[]{:S(2)}, u32[]{:S(2)}) collective-permute-start(bf16[64,1024]{1,0:T(8,128)(2,1)S(1)} %copy.30), channel_id=1, source_target_pairs={{0,4},{4,8},{8,12},{12,16},{16,20},{20,24},{24,28},{28,32},{32,36}... | collective-permute-start | bytes 393224 | tf_op jit(solution)/shard_map/while/body/eval_jaxpr/ppermute | solution.py:11
  73.3 8.1 %collective-permute-start = (bf16[64,1024]{1,0:T(8,128)(2,1)S(1)}, bf16[64,1024]{1,0:T(8,128)(2,1)S(1)}, u32[]{:S(2)}, u32[]{:S(2)}) collective-permute-start(bf16[64,1024]{1,0:T(8,128)(2,1)S(1)} %copy.30), channel_id=1, source_target_pairs={{0,4},{4,8},{8,12},{12,16},{16,20},{20,24},{24,28},{28,32},{32,36}... | collective-permute-start | bytes 393224 | tf_op jit(solution)/shard_map/while/body/eval_jaxpr/ppermute | solution.py:11
  81.4 8.1 %collective-permute-start = (bf16[64,1024]{1,0:T(8,128)(2,1)S(1)}, bf16[64,1024]{1,0:T(8,128)(2,1)S(1)}, u32[]{:S(2)}, u32[]{:S(2)}) collective-permute-start(bf16[64,1024]{1,0:T(8,128)(2,1)S(1)} %copy.30), channel_id=1, source_target_pairs={{0,4},{4,8},{8,12},{12,16},{16,20},{20,24},{24,28},{28,32},{32,36}... | collective-permute-start | bytes 393224 | tf_op jit(solution)/shard_map/while/body/eval_jaxpr/ppermute | solution.py:11
  89.6 8.1 %collective-permute-start = (bf16[64,1024]{1,0:T(8,128)(2,1)S(1)}, bf16[64,1024]{1,0:T(8,128)(2,1)S(1)}, u32[]{:S(2)}, u32[]{:S(2)}) collective-permute-start(bf16[64,1024]{1,0:T(8,128)(2,1)S(1)} %copy.30), channel_id=1, source_target_pairs={{0,4},{4,8},{8,12},{12,16},{16,20},{20,24},{24,28},{28,32},{32,36}... | collective-permute-start | bytes 393224 | tf_op jit(solution)/shard_map/while/body/eval_jaxpr/ppermute | solution.py:11
  97.7 8.1 %collective-permute-start = (bf16[64,1024]{1,0:T(8,128)(2,1)S(1)}, bf16[64,1024]{1,0:T(8,128)(2,1)S(1)}, u32[]{:S(2)}, u32[]{:S(2)}) collective-permute-start(bf16[64,1024]{1,0:T(8,128)(2,1)S(1)} %copy.30), channel_id=1, source_target_pairs={{0,4},{4,8},{8,12},{12,16},{16,20},{20,24},{24,28},{28,32},{32,36}... | collective-permute-start | bytes 393224 | tf_op jit(solution)/shard_map/while/body/eval_jaxpr/ppermute | solution.py:11
  105.8 8.1 %collective-permute-start = (bf16[64,1024]{1,0:T(8,128)(2,1)S(1)}, bf16[64,1024]{1,0:T(8,128)(2,1)S(1)}, u32[]{:S(2)}, u32[]{:S(2)}) collective-permute-start(bf16[64,1024]{1,0:T(8,128)(2,1)S(1)} %copy.30), channel_id=1, source_target_pairs={{0,4},{4,8},{8,12},{12,16},{16,20},{20,24},{24,28},{28,32},{32,36}... | collective-permute-start | bytes 393224 | tf_op jit(solution)/shard_map/while/body/eval_jaxpr/ppermute | solution.py:11
  113.9 8.1 %collective-permute-start = (bf16[64,1024]{1,0:T(8,128)(2,1)S(1)}, bf16[64,1024]{1,0:T(8,128)(2,1)S(1)}, u32[]{:S(2)}, u32[]{:S(2)}) collective-permute-start(bf16[64,1024]{1,0:T(8,128)(2,1)S(1)} %copy.30), channel_id=1, source_target_pairs={{0,4},{4,8},{8,12},{12,16},{16,20},{20,24},{24,28},{28,32},{32,36}... | collective-permute-start | bytes 393224 | tf_op jit(solution)/shard_map/while/body/eval_jaxpr/ppermute | solution.py:11
  122.0 8.6 %collective-permute-start = (bf16[64,1024]{1,0:T(8,128)(2,1)S(1)}, bf16[64,1024]{1,0:T(8,128)(2,1)S(1)}, u32[]{:S(2)}, u32[]{:S(2)}) collective-permute-start(bf16[64,1024]{1,0:T(8,128)(2,1)S(1)} %copy.30), channel_id=1, source_target_pairs={{0,4},{4,8},{8,12},{12,16},{16,20},{20,24},{24,28},{28,32},{32,36}... | collective-permute-start | bytes 393224 | tf_op jit(solution)/shard_map/while/body/eval_jaxpr/ppermute | solution.py:11
  130.6 9.6 %collective-permute-start = (bf16[64,1024]{1,0:T(8,128)(2,1)S(1)}, bf16[64,1024]{1,0:T(8,128)(2,1)S(1)}, u32[]{:S(2)}, u32[]{:S(2)}) collective-permute-start(bf16[64,1024]{1,0:T(8,128)(2,1)S(1)} %copy.30), channel_id=1, source_target_pairs={{0,4},{4,8},{8,12},{12,16},{16,20},{20,24},{24,28},{28,32},{32,36}... | collective-permute-start | bytes 393224 | tf_op jit(solution)/shard_map/while/body/eval_jaxpr/ppermute | solution.py:11
  140.2 8.7 %collective-permute-start = (bf16[64,1024]{1,0:T(8,128)(2,1)S(1)}, bf16[64,1024]{1,0:T(8,128)(2,1)S(1)}, u32[]{:S(2)}, u32[]{:S(2)}) collective-permute-start(bf16[64,1024]{1,0:T(8,128)(2,1)S(1)} %copy.30), channel_id=1, source_target_pairs={{0,4},{4,8},{8,12},{12,16},{16,20},{20,24},{24,28},{28,32},{32,36}... | collective-permute-start | bytes 393224 | tf_op jit(solution)/shard_map/while/body/eval_jaxpr/ppermute | solution.py:11
  148.9 8.1 %collective-permute-start = (bf16[64,1024]{1,0:T(8,128)(2,1)S(1)}, bf16[64,1024]{1,0:T(8,128)(2,1)S(1)}, u32[]{:S(2)}, u32[]{:S(2)}) collective-permute-start(bf16[64,1024]{1,0:T(8,128)(2,1)S(1)} %copy.30), channel_id=1, source_target_pairs={{0,4},{4,8},{8,12},{12,16},{16,20},{20,24},{24,28},{28,32},{32,36}... | collective-permute-start | bytes 393224 | tf_op jit(solution)/shard_map/while/body/eval_jaxpr/ppermute | solution.py:11
  157.1 8.1 %collective-permute-start = (bf16[64,1024]{1,0:T(8,128)(2,1)S(1)}, bf16[64,1024]{1,0:T(8,128)(2,1)S(1)}, u32[]{:S(2)}, u32[]{:S(2)}) collective-permute-start(bf16[64,1024]{1,0:T(8,128)(2,1)S(1)} %copy.30), channel_id=1, source_target_pairs={{0,4},{4,8},{8,12},{12,16},{16,20},{20,24},{24,28},{28,32},{32,36}... | collective-permute-start | bytes 393224 | tf_op jit(solution)/shard_map/while/body/eval_jaxpr/ppermute | solution.py:11
  165.2 8.1 %collective-permute-start = (bf16[64,1024]{1,0:T(8,128)(2,1)S(1)}, bf16[64,1024]{1,0:T(8,128)(2,1)S(1)}, u32[]{:S(2)}, u32[]{:S(2)}) collective-permute-start(bf16[64,1024]{1,0:T(8,128)(2,1)S(1)} %copy.30), channel_id=1, source_target_pairs={{0,4},{4,8},{8,12},{12,16},{16,20},{20,24},{24,28},{28,32},{32,36}... | collective-permute-start | bytes 393224 | tf_op jit(solution)/shard_map/while/body/eval_jaxpr/ppermute | solution.py:11
  173.3 8.1 %collective-permute-start = (bf16[64,1024]{1,0:T(8,128)(2,1)S(1)}, bf16[64,1024]{1,0:T(8,128)(2,1)S(1)}, u32[]{:S(2)}, u32[]{:S(2)}) collective-permute-start(bf16[64,1024]{1,0:T(8,128)(2,1)S(1)} %copy.30), channel_id=1, source_target_pairs={{0,4},{4,8},{8,12},{12,16},{16,20},{20,24},{24,28},{28,32},{32,36}... | collective-permute-start | bytes 393224 | tf_op jit(solution)/shard_map/while/body/eval_jaxpr/ppermute | solution.py:11
  181.4 8.1 %collective-permute-start = (bf16[64,1024]{1,0:T(8,128)(2,1)S(1)}, bf16[64,1024]{1,0:T(8,128)(2,1)S(1)}, u32[]{:S(2)}, u32[]{:S(2)}) collective-permute-start(bf16[64,1024]{1,0:T(8,128)(2,1)S(1)} %copy.30), channel_id=1, source_target_pairs={{0,4},{4,8},{8,12},{12,16},{16,20},{20,24},{24,28},{28,32},{32,36}... | collective-permute-start | bytes 393224 | tf_op jit(solution)/shard_map/while/body/eval_jaxpr/ppermute | solution.py:11
  189.5 8.1 %collective-permute-start = (bf16[64,1024]{1,0:T(8,128)(2,1)S(1)}, bf16[64,1024]{1,0:T(8,128)(2,1)S(1)}, u32[]{:S(2)}, u32[]{:S(2)}) collective-permute-start(bf16[64,1024]{1,0:T(8,128)(2,1)S(1)} %copy.30), channel_id=1, source_target_pairs={{0,4},{4,8},{8,12},{12,16},{16,20},{20,24},{24,28},{28,32},{32,36}... | collective-permute-start | bytes 393224 | tf_op jit(solution)/shard_map/while/body/eval_jaxpr/ppermute | solution.py:11
  197.7 9.1 %collective-permute-start = (bf16[64,1024]{1,0:T(8,128)(2,1)S(1)}, bf16[64,1024]{1,0:T(8,128)(2,1)S(1)}, u32[]{:S(2)}, u32[]{:S(2)}) collective-permute-start(bf16[64,1024]{1,0:T(8,128)(2,1)S(1)} %copy.30), channel_id=1, source_target_pairs={{0,4},{4,8},{8,12},{12,16},{16,20},{20,24},{24,28},{28,32},{32,36}... | collective-permute-start | bytes 393224 | tf_op jit(solution)/shard_map/while/body/eval_jaxpr/ppermute | solution.py:11
  206.8 9.0 %collective-permute-start = (bf16[64,1024]{1,0:T(8,128)(2,1)S(1)}, bf16[64,1024]{1,0:T(8,128)(2,1)S(1)}, u32[]{:S(2)}, u32[]{:S(2)}) collective-permute-start(bf16[64,1024]{1,0:T(8,128)(2,1)S(1)} %copy.30), channel_id=1, source_target_pairs={{0,4},{4,8},{8,12},{12,16},{16,20},{20,24},{24,28},{28,32},{32,36}... | collective-permute-start | bytes 393224 | tf_op jit(solution)/shard_map/while/body/eval_jaxpr/ppermute | solution.py:11
  215.8 8.1 %collective-permute-start = (bf16[64,1024]{1,0:T(8,128)(2,1)S(1)}, bf16[64,1024]{1,0:T(8,128)(2,1)S(1)}, u32[]{:S(2)}, u32[]{:S(2)}) collective-permute-start(bf16[64,1024]{1,0:T(8,128)(2,1)S(1)} %copy.30), channel_id=1, source_target_pairs={{0,4},{4,8},{8,12},{12,16},{16,20},{20,24},{24,28},{28,32},{32,36}... | collective-permute-start | bytes 393224 | tf_op jit(solution)/shard_map/while/body/eval_jaxpr/ppermute | solution.py:11
  264.5 8.8 %collective-permute-start = (bf16[64,1024]{1,0:T(8,128)(2,1)S(1)}, bf16[64,1024]{1,0:T(8,128)(2,1)S(1)}, u32[]{:S(2)}, u32[]{:S(2)}) collective-permute-start(bf16[64,1024]{1,0:T(8,128)(2,1)S(1)} %copy.30), channel_id=1, source_target_pairs={{0,4},{4,8},{8,12},{12,16},{16,20},{20,24},{24,28},{28,32},{32,36}... | collective-permute-start | bytes 393224 | tf_op jit(solution)/shard_map/while/body/eval_jaxpr/ppermute | solution.py:11
  273.3 9.4 %collective-permute-start = (bf16[64,1024]{1,0:T(8,128)(2,1)S(1)}, bf16[64,1024]{1,0:T(8,128)(2,1)S(1)}, u32[]{:S(2)}, u32[]{:S(2)}) collective-permute-start(bf16[64,1024]{1,0:T(8,128)(2,1)S(1)} %copy.30), channel_id=1, source_target_pairs={{0,4},{4,8},{8,12},{12,16},{16,20},{20,24},{24,28},{28,32},{32,36}... | collective-permute-start | bytes 393224 | tf_op jit(solution)/shard_map/while/body/eval_jaxpr/ppermute | solution.py:11
  282.8 8.5 %collective-permute-start = (bf16[64,1024]{1,0:T(8,128)(2,1)S(1)}, bf16[64,1024]{1,0:T(8,128)(2,1)S(1)}, u32[]{:S(2)}, u32[]{:S(2)}) collective-permute-start(bf16[64,1024]{1,0:T(8,128)(2,1)S(1)} %copy.30), channel_id=1, source_target_pairs={{0,4},{4,8},{8,12},{12,16},{16,20},{20,24},{24,28},{28,32},{32,36}... | collective-permute-start | bytes 393224 | tf_op jit(solution)/shard_map/while/body/eval_jaxpr/ppermute | solution.py:11
  (13 other events, 121.8 us)
Sparse Core Ops, SparseCore 0:
  19.7 40.8 reduce-scatter.1
  430.4 51.4 all-reduce.4
where the time goes:
time: 491 us; the launch traced here: 490 us
  waiting for transfers between devices  291 us (59%)
  blocking collectives  143 us (29%)
  matrix products  21.5 us (4%)
  between operations  14.2 us (3%)
  local copies, waits for them, and re-layouts  14 us (3%)
    ppermute x31, waiting for transfers between devices, shifted(): lax.ppermute(array, axis, [(i, (i + by) % devices) for i in range(devices)])  239 us
    unnamed x1, blocking collectives  64.3 us
    psum x1, waiting for transfers between devices, on_device(): totals = lax.psum(partial_scores, 'tensor')  51.6 us
    psum x1, blocking collectives, on_device(): train_sq, query_sq = lax.psum((train_sq, query_sq), 'tensor')  40.7 us
    psum x1, blocking collectives, on_device(): in_full = lax.psum(part_in, 'tensor')  37.8 us
    dot_general x1, matrix products, on_device(): jnp.dot(out_grads.reshape(train_rows * seq_len, out_grads.shape[2]), proj...  11.9 us
    dynamic_update_slice x32, local copies, waits for them, and re-layouts, place_query(): lax.dynamic_update_slice_in_dim(buffer, inner(train_grads, block), owner...  11.9 us
  transfers between devices with their start and end apart: 33, of which 32 were waited for; matrix products, arithmetic and copies ran while one was open for 4% of the time, Pallas kernels for 0%

commit v1 on v0

v1 whole, which is shorter than its diff:
```python
import jax
import jax.numpy as jnp
from jax import lax
from jax.experimental import pallas as pl
from jax.experimental.pallas import tpu as pltpu
from jax.sharding import PartitionSpec as P

eps = 1e-06
f32 = jnp.float32
bf16 = jnp.bfloat16
MESH = pl.DeviceIdType.MESH

SIDE = 4
CHUNKS = 8
AHEAD = 3
ENTER = 1
REDUCE_LAG = 2
QUERY_STEPS = (2,5,6,7)
LAG = 7
RING = ((2, 0), (2, 1), (1, 0), (1, 1), (3, 0), (3, 1), (0, 1))
AROUND = (1, 3, 2)


def dot(left, right):
    return jnp.dot(left, right, preferred_element_type=f32)


def kernel(
    lengths_in, out_grads, activations, proj_in_in, proj_out_in, queries_in,
    scores,
    lengths, query_grads, proj_in_t, proj_out_t, out_held, act_held, w_out, w_in,
    own_part, pair_send, pair_recv, reduce_send, reduce_recv,
    grads_send, grads_recv, grads_wide, train,
    queries, square_part, square_send, square_recv,
    part_send, part_recv, part_rows, spread,
    small_sem, load_sem, pair_ssem, pair_rsem, reduce_ssem, reduce_rsem,
    grads_ssem, grads_rsem, swap_sem,
    qa_ssem, qa_rsem, qb_ssem, qb_rsem,
    square_ssem, square_rsem, part_ssem, part_rsem,
):
    dp = lax.axis_index("dp")
    tensor = lax.axis_index("tensor")
    x, y, z_lo = dp // 8, (dp // 2) % 4, dp % 2
    z_hi, core = tensor // 2, tensor % 2
    z = z_hi * 2 + z_lo
    here = x * SIDE + y

    def device(x, y, z, core):
        return (x * 8 + y * 2 + z % 2, (z // 2) * 2 + core)

    def ring_peer(step_z, step_core):
        return (z + step_z) % SIDE, (core + step_core) % 2

    def grads_place(z, core):
        return 1 - z % 2, core * 2 + z // 2

    def part_place(z, core):
        return (z // 2) * 4 + (z % 2) * 2 + core

    sibling = device(x, y, z, 1 - core)
    ring = [ring_peer(*steps) for steps in RING]
    ring_ids = [device(x, y, *peer) for peer in ring]
    x_ids = [device((x + step) % SIDE, y, z, core) for step in AROUND]
    y_ids = [device(x, (y + step) % SIDE, z, core) for step in AROUND]

    def remote(src, dst, send_sem, recv_sem, to):
        return pltpu.make_async_remote_copy(
            src_ref=src, dst_ref=dst, send_sem=send_sem, recv_sem=recv_sem,
            device_id=to, device_id_type=MESH,
        )

    def loads(chunk):
        for half in range(2):
            rows = pl.ds(pl.multiple_of((core + half) % 2 * 256, 256), 256)
            held = pl.ds(half * 256, 256)
            yield pltpu.make_async_copy(
                out_grads.at[chunk, rows], out_held.at[chunk, held], load_sem.at[chunk * 4 + half]
            )
            yield pltpu.make_async_copy(
                activations.at[chunk, rows], act_held.at[chunk, held], load_sem.at[chunk * 4 + 2 + half]
            )

    small = [
        pltpu.make_async_copy(proj_out_in, proj_out_t, small_sem.at[0]),
        pltpu.make_async_copy(proj_in_in, proj_in_t, small_sem.at[1]),
        pltpu.make_async_copy(lengths_in, lengths, small_sem.at[2]),
        pltpu.make_async_copy(queries_in, query_grads, small_sem.at[3]),
    ]
    for load in small:
        load.start()
    for load in small:
        load.wait()
    for chunk in range(AHEAD):
        for load in loads(chunk):
            load.start()

    barrier = pltpu.get_barrier_semaphore()
    peers = ring_ids + x_ids + y_ids
    for peer in peers:
        pl.semaphore_signal(barrier, inc=1, device_id=peer, device_id_type=MESH)

    rank_row = lax.broadcasted_iota(jnp.int32, (64, 128), 0)
    lane = lax.broadcasted_iota(jnp.int32, (64, 128), 1)
    place_out = (lane == (rank_row % 2) * 32 + rank_row // 2).astype(bf16)
    place_in = (lane == rank_row + 64).astype(bf16)
    columns = (((0,), (0,)), ((), ()))
    w_in[...] = lax.dot_general(proj_in_t[...], place_in, columns, preferred_element_type=f32).astype(bf16)
    w_out[...] = lax.dot_general(proj_out_t[...], place_out, columns, preferred_element_type=f32).astype(bf16)

    half_columns = pl.ds(pl.multiple_of(core * 1024, 1024), 1024)
    swap_out = remote(
        query_grads.at[pl.ds(pl.multiple_of((1 - core) * 32, 32), 32)],
        queries.at[here, :, half_columns],
        swap_sem.at[0], swap_sem.at[1], sibling,
    )
    swap_own = pltpu.make_async_copy(
        query_grads.at[pl.ds(pl.multiple_of(core * 32, 32), 32)],
        queries.at[here, :, half_columns],
        swap_sem.at[2],
    )

    def query_half(half, owner, ssem, rsem, index, to):
        rows = queries.at[owner, pl.ds(half * 16, 16)]
        return remote(rows, rows, ssem.at[index], rsem.at[owner], to)

    def a_send(index, owner, to):
        return query_half(0, owner, qa_ssem, qa_rsem, index, to)

    def b_send(index, owner, to):
        return query_half(1, owner, qb_ssem, qb_rsem, index, to)

    def enter():
        pl.semaphore_wait(barrier, len(peers))
        swap_out.start()
        swap_own.start()
        for chunk in range(ENTER + 1):
            pair_copy(chunk).start()

    def queries_first():
        swap_own.wait()
        swap_out.wait()
        for i in range(3):
            a_send(i, here, x_ids[i]).start()
            b_send(i, here, y_ids[i]).start()
        for i in range(3):
            a_send(3 + i, here, y_ids[i]).start()
            b_send(3 + i, here, x_ids[i]).start()

    def queries_second(k):
        step = AROUND[k]
        a_owner = ((x + step) % SIDE) * SIDE + y
        a_send(0, a_owner, sibling).wait_recv()
        for i in range(3):
            a_send(6 + k * 3 + i, a_owner, y_ids[i]).start()
        b_owner = x * SIDE + (y + step) % SIDE
        b_send(0, b_owner, sibling).wait_recv()
        for i in range(3):
            b_send(6 + k * 3 + i, b_owner, x_ids[i]).start()

    def queries_last():
        for step in AROUND:
            for other in (0,) + AROUND:
                a_owner = ((x + other) % SIDE) * SIDE + (y + step) % SIDE
                a_send(0, a_owner, sibling).wait_recv()
                b_owner = ((x + step) % SIDE) * SIDE + (y + other) % SIDE
                b_send(0, b_owner, sibling).wait_recv()

    token = lax.broadcasted_iota(jnp.int32, (128, 128), 0)

    def pair_copy(chunk):
        return remote(pair_send.at[chunk], pair_recv.at[chunk], pair_ssem.at[chunk], pair_rsem.at[chunk], sibling)

    def reduce_copy(chunk, owner_hi, source_hi):
        to = device(x, y, owner_hi * 2 + 1 - z_lo, core)
        return remote(
            reduce_send.at[chunk, owner_hi], reduce_recv.at[chunk, source_hi],
            reduce_ssem.at[chunk * 2 + owner_hi], reduce_rsem.at[chunk * 2 + source_hi], to,
        )

    def project(chunk):
        for load in loads(chunk):
            load.wait()

        @pl.when(chunk + AHEAD < CHUNKS)
        def _():
            for load in loads(chunk + AHEAD):
                load.start()

        total = dot(out_held[chunk], w_out[...])
        total += dot(act_held[chunk], w_in[...])
        kept = []
        for place in range(4):
            owner = ((core + place // 2) % 2) * 2 + place % 2
            length = lengths[chunk * 4 + owner]
            kept.append(jnp.where(token < length, total[place * 128 : place * 128 + 128], 0.0))
        own_part[chunk, 0:128] = kept[0]
        own_part[chunk, 128:256] = kept[1]
        pair_send[chunk, 0:128] = kept[2]
        pair_send[chunk, 128:256] = kept[3]
    def reduce(chunk):
        pair_copy(chunk).wait_recv()
        for owner_hi in range(2):
            rows = slice(owner_hi * 128, owner_hi * 128 + 128)
            total = own_part[chunk, rows] + pair_recv[chunk, rows]
            largest = jnp.max(jnp.abs(total), axis=0, keepdims=True)
            power = jnp.floor(jnp.log2(jnp.maximum(largest, 1e-30))) + 1.0
            scaled = jnp.round(total * jnp.exp2(15.0 - power))
            coded = jnp.clip(scaled, -32767.0, 32767.0).astype(jnp.int32).astype(jnp.int16)
            reduce_send[chunk, owner_hi, 0:128] = coded
            reduce_send[chunk, owner_hi, 128:144] = jnp.broadcast_to(power, (16, 128)).astype(jnp.int32).astype(jnp.int16)
            reduce_copy(chunk, owner_hi, z_hi).start()

    def outer(chunk):
        for source_hi in range(2):
            reduce_copy(chunk, 0, source_hi).wait_recv()
        total = jnp.zeros((128, 128), f32)
        for source_hi in range(2):
            power = reduce_recv[chunk, source_hi, 128:144].astype(jnp.int32)[0:1].astype(f32)
            total += reduce_recv[chunk, source_hi, 0:128].astype(jnp.int32).astype(f32) * jnp.exp2(power - 15.0)
        sides = total.astype(bf16)
        wide = sides.astype(f32)
        lanes = lax.broadcasted_iota(jnp.int32, (128, 128), 1)
        in_twice = jnp.where(lanes < 64, pltpu.roll(wide, 64, 1), wide).astype(bf16)
        both = lax.dot_general(sides, in_twice, columns, preferred_element_type=f32)
        grads = jnp.where(lanes[0:32] < 64, both[0:32], both[32:64])
        squares = jnp.square(grads.astype(bf16).astype(f32))
        square = jnp.sum(jnp.sum(squares, axis=0, keepdims=True), axis=1, keepdims=True)
        scaled = (grads * (64.0 * lax.rsqrt(square + eps))).astype(bf16)
        grads_send[0, chunk] = scaled[0:16]
        grads_send[1, chunk] = scaled[16:32]

    def grads_copy(batch, index, peer, source, to):
        block, owner = source
        rows = pl.ds(batch * 4, 4)
        return remote(
            grads_send.at[peer[0] // 2, rows], grads_recv.at[block, rows, owner],
            grads_ssem.at[batch * 7 + index], grads_rsem.at[batch * 8 + block * 4 + owner], to,
        )

    def grads_out(batch):
        for i in range(7):
            grads_copy(batch, i, ring[i], grads_place(z, core), ring_ids[i]).start()

    def step(s, carry):
        pl.when(s < CHUNKS)(lambda: project(s))
        pl.when(s == ENTER)(enter)
        pl.when((s > ENTER) & (s < CHUNKS))(lambda: pair_copy(s).start())
        pl.when(s == QUERY_STEPS[0])(queries_first)
        pl.when((s >= REDUCE_LAG) & (s < CHUNKS + REDUCE_LAG))(lambda: reduce(s - REDUCE_LAG))
        for k in range(3):
            pl.when(s == QUERY_STEPS[1 + k])(lambda: queries_second(k))
        pl.when(s >= LAG)(lambda: outer(s - LAG))
        pl.when(s == LAG + 3)(lambda: grads_out(0))
        pl.when(s == LAG + 7)(lambda: grads_out(1))
        return carry

    lax.fori_loop(0, CHUNKS + LAG, step, 0)

    spread[...] = jnp.zeros_like(spread)
    query_row = lax.broadcasted_iota(jnp.int32, (32, 128), 0)
    query_lane = lax.broadcasted_iota(jnp.int32, (32, 128), 1)
    for source in range(8):
        at = ((source // 2) % 2) * 64 + (source % 2) * 32
        pattern = (query_lane == query_row + at).astype(bf16)
        for column in range(4):
            spread[source * 128 + column * 32 : source * 128 + column * 32 + 32, column * 128 : column * 128 + 128] = pattern

    queries_last()

    def square_rows(block, carry):
        wide = queries[block].astype(f32)
        squares = wide * wide
        total = squares[:, 0:128]
        for column in range(1, 16):
            total += squares[:, column * 128 : column * 128 + 128]
        square_part[pl.ds(pl.multiple_of(block * 32, 32), 32)] = total
        return carry

    lax.fori_loop(0, 16, square_rows, 0)
    row = lax.broadcasted_iota(jnp.int32, (8, 128), 0)
    squares = jnp.zeros((8, 128), f32)
    for group in range(4):
        sums = lax.dot_general(
            jnp.ones((8, 128), f32), square_part[group * 128 : group * 128 + 128], (((1,), (1,)), ((), ())),
            precision=lax.Precision.HIGHEST, preferred_element_type=f32,
        )
        squares = jnp.where(row == group, sums, squares)
    square_send[...] = squares

    def square_copy(index, place, to):
        return remote(square_send, square_recv.at[place], square_ssem.at[index], square_rsem.at[place], to)

    own_place = part_place(z, core)
    for i in range(7):
        square_copy(i, own_place, ring_ids[i]).start()
    square_recv[own_place] = squares

    own_grads = grads_place(z, core)
    for n in range(CHUNKS):
        grads_recv[own_grads[0], n, own_grads[1]] = grads_send[z_hi, n]
    for batch in range(2):
        for i in range(7):
            grads_copy(batch, i, ring[i], grads_place(*ring[i]), ring_ids[i]).wait_recv()
    grads_wide[...] = grads_recv[...].reshape(1024, 128).astype(f32)
    for j in range(16):
        train[:, j * 128 : j * 128 + 128] = grads_wide[pl.ds(j, 64, stride=16), :].astype(bf16)

    products = lax.dot_general(
        train[...], queries[...].reshape(512, 2048), (((1,), (1,)), ((), ())), preferred_element_type=f32
    )
    part_send[...] = products.astype(bf16).reshape(2, 32, 512)

    def part_copy(index, peer, place, to):
        return remote(
            part_send.at[peer[0] % 2], part_recv.at[place], part_ssem.at[index], part_rsem.at[place], to
        )

    for i in range(7):
        part_copy(i, ring[i], own_place, ring_ids[i]).start()
    part_recv[own_place] = part_send[z_lo]

    for chunk in range(CHUNKS):
        pair_copy(chunk).wait_send()
        for owner_hi in range(2):
            reduce_copy(chunk, owner_hi, 0).wait_send()
    for batch in range(2):
        for i in range(7):
            grads_copy(batch, i, ring[i], own_grads, ring_ids[i]).wait_send()
    for i in range(15):
        a_send(i, here, sibling).wait_send()
        b_send(i, here, sibling).wait_send()
    for i in range(7):
        square_copy(i, own_place, ring_ids[i]).wait_send()

    for i in range(7):
        square_copy(i, part_place(*ring[i]), ring_ids[i]).wait_recv()
    left = jnp.concatenate([square_recv[place] for place in range(8)], axis=1)
    pieces = []
    for _ in range(3):
        piece = left.astype(bf16)
        pieces.append(piece)
        left = left - piece.astype(f32)
    spread_squares = sum(dot(piece, spread[...]) for piece in pieces)
    scales = lax.rsqrt(spread_squares + eps)

    for i in range(7):
        part_copy(i, ring[i], part_place(*ring[i]), ring_ids[i]).wait_recv()
    for place in range(8):
        for group in range(4):
            part_rows[group * 32 : group * 32 + 32, place * 128 : place * 128 + 128] = part_recv[
                place, :, group * 128 : group * 128 + 128
            ]
    result = dot(part_rows[...], spread[...])
    for group in range(4):
        scores[:, group * 512 : group * 512 + 512] = result[group * 32 : group * 32 + 32] * scales[group : group + 1]
    for i in range(7):
        part_copy(i, ring[i], own_place, ring_ids[i]).wait_send()


def on_device(activations, out_grads, lengths, proj_in, proj_out, query_grads):
    dma = pltpu.SemaphoreType.DMA
    vmem = pl.BlockSpec(memory_space=pltpu.VMEM)
    hbm = pl.BlockSpec(memory_space=pltpu.HBM)
    return pl.pallas_call(
        kernel,
        out_shape=jax.ShapeDtypeStruct((32, 2048), f32),
        in_specs=[hbm] * 6,
        out_specs=vmem,
        scratch_shapes=[
            pltpu.SMEM((32,), jnp.int32),
            pltpu.VMEM((64, 1024), bf16),
            pltpu.VMEM((64, 512), bf16),
            pltpu.VMEM((64, 2048), bf16),
            pltpu.VMEM((8, 512, 2048), bf16),
            pltpu.VMEM((8, 512, 512), bf16),
            pltpu.VMEM((2048, 128), bf16),
            pltpu.VMEM((512, 128), bf16),
            pltpu.VMEM((8, 256, 128), f32),
            pltpu.VMEM((8, 256, 128), f32),
            pltpu.VMEM((8, 256, 128), f32),
            pltpu.VMEM((8, 2, 144, 128), jnp.int16),
            pltpu.VMEM((8, 2, 144, 128), jnp.int16),
            pltpu.VMEM((2, 8, 16, 128), bf16),
            pltpu.VMEM((2, 8, 4, 16, 128), bf16),
            pltpu.VMEM((1024, 128), f32),
            pltpu.VMEM((64, 2048), bf16),
            pltpu.VMEM((16, 32, 2048), bf16),
            pltpu.VMEM((512, 128), f32),
            pltpu.VMEM((8, 128), f32),
            pltpu.VMEM((8, 8, 128), f32),
            pltpu.VMEM((2, 32, 512), bf16),
            pltpu.VMEM((8, 32, 512), bf16),
            pltpu.VMEM((128, 1024), bf16),
            pltpu.VMEM((1024, 512), bf16),
            dma((4,)),
            dma((32,)),
            dma((8,)),
            dma((8,)),
            dma((16,)),
            dma((16,)),
            dma((14,)),
            dma((16,)),
            dma((3,)),
            dma((15,)),
            dma((16,)),
            dma((15,)),
            dma((16,)),
            dma((7,)),
            dma((8,)),
            dma((7,)),
            dma((8,)),
        ],
        compiler_params=pltpu.CompilerParams(
            collective_id=0, has_side_effects=True, vmem_limit_bytes=64 * 2**20 - 512 * 1024
        ),
    )(
        lengths,
        out_grads.reshape(8, 512, 2048),
        activations.reshape(8, 512, 512),
        proj_in.T,
        proj_out.T,
        query_grads,
    )


def solution(mesh):
    placed = (
        P("dp", None, "tensor"),
        P("dp", None, "tensor"),
        P("dp"),
        P("tensor", None),
        P("tensor", None),
        P("dp", "tensor"),
    )
    return jax.shard_map(
        on_device, mesh=mesh, in_specs=placed, out_specs=P("dp", None), check_vma=False
    )
```

time: 491 us -> 38.7 us (0.08)
  waiting for transfers between devices: 291 us -> 0 us
  blocking collectives: 143 us -> 0 us
  Pallas kernels: 0 us -> 36.9 us
  matrix products: 21.5 us -> 0 us
  between operations: 14.2 us -> 0.01 us
  local copies, waits for them, and re-layouts: 14 us -> 1.67 us
    ppermute x31 -> x0, waiting for transfers between devices: 239 us -> none  [shifted(): lax.ppermute(array, axis, [(i, (i + by) % devices) for i in range(devices)])]
    psum x2 -> x0, blocking collectives: 78.5 us -> none  [the longest x1 40.7 us: on_device(): train_sq, query_sq = lax.psum((train_sq, query_sq), 'tensor')]
    unnamed x1 -> x0, blocking collectives: 64.3 us -> none
    psum x1 -> x0, waiting for transfers between devices: 51.6 us -> none  [on_device(): totals = lax.psum(partial_scores, 'tensor')]
    pallas_call x0 -> x1, Pallas kernels: none -> 36.9 us  [on_device(): pl.pallas_call(kernel, out_shape=jax.ShapeDtypeStruct((32, 2048), f32), i...]
    dot_general x35 -> x0, matrix products: 21.5 us -> none  [the longest x1 11.9 us: on_device(): jnp.dot(out_grads.reshape(train_rows * seq_len, out_grads.shape[2]), proj...]
    dynamic_update_slice x32 -> x0, local copies, waits for them, and re-layouts: 11.9 us -> none  [place_query(): lax.dynamic_update_slice_in_dim(buffer, inner(train_grads, block), owner...]
  transfers between devices with their start and end apart: 33 -> 0, of which waited for: 32 -> 0; matrix products, arithmetic and copies ran while one was open for 4% -> 0% of each run, Pallas kernels for 0% -> 0%
where the time goes in v1:
time: 38.7 us; the launch traced here: 38.6 us
  Pallas kernels  36.9 us (95%)
  local copies, waits for them, and re-layouts  1.67 us (4%)
    pallas_call x1, Pallas kernels, on_device(): pl.pallas_call(kernel, out_shape=jax.ShapeDtypeStruct((32, 2048), f32), i...  36.9 us
    unnamed x1, local copies, waits for them, and re-layouts  1.67 us

profile of v1, /device:TPU:1, one launch (start us, length us, event | category | flops | bytes accessed | tf_op | source)
XLA Modules:
  0.0 38.6 jit_solution(15027946636160142753)
XLA Ops:
  0.0 36.9 %shard_map.64 = f32[32,2048]{1,0:T(8,128)} custom-call(s32[32]{0:T(128)} %lengths_in.1, bf16[8,512,2048]{2,1,0:T(8,128)(2,1)} %bitcast.4, bf16[8,512,512]{2,1,0:T(8,128)(2,1)} %bitcast.5, bf16[64,512]{1,0:T(8,128)(2,1)} %bitcast.7, bf16[64,2048]{1,0:T(8,128)(2,1)} %bitcast.6, bf16[64,1024]{1,0:T(8,128)(2,1)} %queries_in.1), custom_call_target="tpu_custom_call" | custom-call | tf_op jit(solution)/shard_map/pallas_call | solution.py:364
  36.9 1.7 %copy.8 = f32[32,2048]{1,0:T(8,128)} copy(f32[32,2048]{1,0:T(8,128)} %shard_map.64) | data formatting | bytes 524288

commit v2 on v1

--- a/solution.py
+++ b/solution.py
@@ -1,3 +1,5 @@
+import functools
+
 import jax
 import jax.numpy as jnp
 from jax import lax
@@ -13,12 +15,11 @@
 SIDE = 4
 CHUNKS = 8
 AHEAD = 3
-ENTER = 1
 REDUCE_LAG = 2
-QUERY_STEPS = (2,5,6,7)
+QUERY_STEPS = (1, 5, 8, 10, 12)
+BATCHES = ((0, 4), (4, 7), (7, 8))
 LAG = 7
 RING = ((2, 0), (2, 1), (1, 0), (1, 1), (3, 0), (3, 1), (0, 1))
-AROUND = (1, 3, 2)
 
 
 def dot(left, right):
@@ -35,7 +36,7 @@
     part_send, part_recv, part_rows, spread,
     small_sem, load_sem, pair_ssem, pair_rsem, reduce_ssem, reduce_rsem,
     grads_ssem, grads_rsem, swap_sem,
-    qa_ssem, qa_rsem, qb_ssem, qb_rsem,
+    query_ssem, query_rsem,
     square_ssem, square_rsem, part_ssem, part_rsem,
 ):
     dp = lax.axis_index("dp")
@@ -60,14 +61,19 @@
     sibling = device(x, y, z, 1 - core)
     ring = [ring_peer(*steps) for steps in RING]
     ring_ids = [device(x, y, *peer) for peer in ring]
-    x_ids = [device((x + step) % SIDE, y, z, core) for step in AROUND]
-    y_ids = [device(x, (y + step) % SIDE, z, core) for step in AROUND]
+    around_ids = [device((x + step) % SIDE, y, z, core) for step in (1, 2, 3)]
+    around_ids += [device(x, (y + step) % SIDE, z, core) for step in (1, 2, 3)]
 
     def remote(src, dst, send_sem, recv_sem, to):
         return pltpu.make_async_remote_copy(
             src_ref=src, dst_ref=dst, send_sem=send_sem, recv_sem=recv_sem,
             device_id=to, device_id_type=MESH,
         )
+
+    barrier = pltpu.get_barrier_semaphore()
+    peers = ring_ids + around_ids
+    for peer in peers:
+        pl.semaphore_signal(barrier, inc=1, device_id=peer, device_id_type=MESH)
 
     def loads(chunk):
         for half in range(2):
@@ -86,18 +92,13 @@
         pltpu.make_async_copy(lengths_in, lengths, small_sem.at[2]),
         pltpu.make_async_copy(queries_in, query_grads, small_sem.at[3]),
     ]
-    for load in small:
+    for load in small + list(loads(0)):
         load.start()
     for load in small:
         load.wait()
-    for chunk in range(AHEAD):
+    for chunk in range(1, AHEAD):
         for load in loads(chunk):
             load.start()
-
-    barrier = pltpu.get_barrier_semaphore()
-    peers = ring_ids + x_ids + y_ids
-    for peer in peers:
-        pl.semaphore_signal(barrier, inc=1, device_id=peer, device_id_type=MESH)
 
     rank_row = lax.broadcasted_iota(jnp.int32, (64, 128), 0)
     lane = lax.broadcasted_iota(jnp.int32, (64, 128), 1)
@@ -119,51 +120,62 @@
         swap_sem.at[2],
     )
 
-    def query_half(half, owner, ssem, rsem, index, to):
-        rows = queries.at[owner, pl.ds(half * 16, 16)]
-        return remote(rows, rows, ssem.at[index], rsem.at[owner], to)
-
-    def a_send(index, owner, to):
-        return query_half(0, owner, qa_ssem, qa_rsem, index, to)
-
-    def b_send(index, owner, to):
-        return query_half(1, owner, qb_ssem, qb_rsem, index, to)
-
-    def enter():
-        pl.semaphore_wait(barrier, len(peers))
-        swap_out.start()
-        swap_own.start()
-        for chunk in range(ENTER + 1):
-            pair_copy(chunk).start()
-
-    def queries_first():
+    pl.semaphore_wait(barrier, len(peers))
+    swap_out.start()
+    swap_own.start()
+
+    def at(way, along, across):
+        step_x, step_y = (along, across) if way == 0 else (across, along)
+        return (x + step_x) % SIDE, (y + step_y) % SIDE
+
+    def query_copy(way, owner, columns, index, to):
+        rows = queries.at[owner[0] * SIDE + owner[1], pl.ds(way * 16, 16), columns]
+        return remote(
+            rows, rows, query_ssem.at[way * 19 + index], query_rsem.at[way * 16 + owner[0] * SIDE + owner[1]],
+            device(*to, z, core),
+        )
+
+    every = pl.ds(0, 2048)
+
+    def query_wait(way, along, across):
+        query_copy(way, at(way, along, across), every, 0, at(way, 1, 0)).wait_recv()
+
+    def spread_first():
         swap_own.wait()
         swap_out.wait()
-        for i in range(3):
-            a_send(i, here, x_ids[i]).start()
-            b_send(i, here, y_ids[i]).start()
-        for i in range(3):
-            a_send(3 + i, here, y_ids[i]).start()
-            b_send(3 + i, here, x_ids[i]).start()
-
-    def queries_second(k):
-        step = AROUND[k]
-        a_owner = ((x + step) % SIDE) * SIDE + y
-        a_send(0, a_owner, sibling).wait_recv()
-        for i in range(3):
-            a_send(6 + k * 3 + i, a_owner, y_ids[i]).start()
-        b_owner = x * SIDE + (y + step) % SIDE
-        b_send(0, b_owner, sibling).wait_recv()
-        for i in range(3):
-            b_send(6 + k * 3 + i, b_owner, x_ids[i]).start()
-
-    def queries_last():
-        for step in AROUND:
-            for other in (0,) + AROUND:
-                a_owner = ((x + other) % SIDE) * SIDE + (y + step) % SIDE
-                a_send(0, a_owner, sibling).wait_recv()
-                b_owner = ((x + step) % SIDE) * SIDE + (y + other) % SIDE
-                b_send(0, b_owner, sibling).wait_recv()
+        for index, along in enumerate((1, 3, 2)):
+            for way in range(2):
+                query_copy(way, at(way, 0, 0), every, index, at(way, along, 0)).start()
+        for way in range(2):
+            spread_second(way, 0)
+
+    def spread_second(way, along):
+        query_copy(way, at(way, along, 0), every, 3 + along * 4, at(way, 0, 1)).start()
+        query_copy(way, at(way, along, 0), every, 4 + along * 4, at(way, 0, 3)).start()
+
+    def pass_first():
+        for along in (1, 3, 2):
+            for way in range(2):
+                query_wait(way, along, 0)
+                spread_second(way, along)
+
+    def pass_second(along):
+        for way in range(2):
+            query_wait(way, along, 3)
+            query_copy(way, at(way, along, 3), pl.ds(0, 1024), 5 + along * 4, at(way, 0, 1)).start()
+            query_wait(way, along, 1)
+            query_copy(way, at(way, along, 1), pl.ds(1024, 1024), 6 + along * 4, at(way, 0, 3)).start()
+
+    def opposite_second():
+        for along in range(4):
+            for way in range(2):
+                query_wait(way, along, 2)
+
+    def pass_both():
+        pass_second(1)
+        pass_second(3)
+
+    query_steps = (spread_first, pass_first, lambda: pass_second(0), pass_both, lambda: pass_second(2))
 
     token = lax.broadcasted_iota(jnp.int32, (128, 128), 0)
 
@@ -197,6 +209,7 @@
         own_part[chunk, 128:256] = kept[1]
         pair_send[chunk, 0:128] = kept[2]
         pair_send[chunk, 128:256] = kept[3]
+        pair_copy(chunk).start()
     def reduce(chunk):
         pair_copy(chunk).wait_recv()
         for owner_hi in range(2):
@@ -231,7 +244,8 @@
 
     def grads_copy(batch, index, peer, source, to):
         block, owner = source
-        rows = pl.ds(batch * 4, 4)
+        first, last = BATCHES[batch]
+        rows = pl.ds(first, last - first)
         return remote(
             grads_send.at[peer[0] // 2, rows], grads_recv.at[block, rows, owner],
             grads_ssem.at[batch * 7 + index], grads_rsem.at[batch * 8 + block * 4 + owner], to,
@@ -243,15 +257,13 @@
 
     def step(s, carry):
         pl.when(s < CHUNKS)(lambda: project(s))
-        pl.when(s == ENTER)(enter)
-        pl.when((s > ENTER) & (s < CHUNKS))(lambda: pair_copy(s).start())
-        pl.when(s == QUERY_STEPS[0])(queries_first)
+        pl.when(s == QUERY_STEPS[0])(spread_first)
         pl.when((s >= REDUCE_LAG) & (s < CHUNKS + REDUCE_LAG))(lambda: reduce(s - REDUCE_LAG))
-        for k in range(3):
-            pl.when(s == QUERY_STEPS[1 + k])(lambda: queries_second(k))
+        for k in range(1, 5):
+            pl.when(s == QUERY_STEPS[k])(query_steps[k])
         pl.when(s >= LAG)(lambda: outer(s - LAG))
-        pl.when(s == LAG + 3)(lambda: grads_out(0))
-        pl.when(s == LAG + 7)(lambda: grads_out(1))
+        for batch, (first, last) in enumerate(BATCHES):
+            pl.when(s == LAG + last - 1)(functools.partial(grads_out, batch))
         return carry
 
     lax.fori_loop(0, CHUNKS + LAG, step, 0)
@@ -260,12 +272,14 @@
     query_row = lax.broadcasted_iota(jnp.int32, (32, 128), 0)
     query_lane = lax.broadcasted_iota(jnp.int32, (32, 128), 1)
     for source in range(8):
-        at = ((source // 2) % 2) * 64 + (source % 2) * 32
-        pattern = (query_lane == query_row + at).astype(bf16)
+        shift = ((source // 2) % 2) * 64 + (source % 2) * 32
+        pattern = (query_lane == query_row + shift).astype(bf16)
         for column in range(4):
             spread[source * 128 + column * 32 : source * 128 + column * 32 + 32, column * 128 : column * 128 + 128] = pattern
 
-    queries_last()
+    opposite_second()
+
+    own_place = part_place(z, core)
 
     def square_rows(block, carry):
         wide = queries[block].astype(f32)
@@ -277,20 +291,19 @@
         return carry
 
     lax.fori_loop(0, 16, square_rows, 0)
+    sums = lax.dot_general(
+        jnp.ones((8, 128), f32), square_part[...], (((1,), (1,)), ((), ())),
+        precision=lax.Precision.HIGHEST, preferred_element_type=f32,
+    )
     row = lax.broadcasted_iota(jnp.int32, (8, 128), 0)
     squares = jnp.zeros((8, 128), f32)
     for group in range(4):
-        sums = lax.dot_general(
-            jnp.ones((8, 128), f32), square_part[group * 128 : group * 128 + 128], (((1,), (1,)), ((), ())),
-            precision=lax.Precision.HIGHEST, preferred_element_type=f32,
-        )
-        squares = jnp.where(row == group, sums, squares)
+        squares = jnp.where(row == group, sums[:, group * 128 : group * 128 + 128], squares)
     square_send[...] = squares
 
     def square_copy(index, place, to):
         return remote(square_send, square_recv.at[place], square_ssem.at[index], square_rsem.at[place], to)
 
-    own_place = part_place(z, core)
     for i in range(7):
         square_copy(i, own_place, ring_ids[i]).start()
     square_recv[own_place] = squares
@@ -298,7 +311,7 @@
     own_grads = grads_place(z, core)
     for n in range(CHUNKS):
         grads_recv[own_grads[0], n, own_grads[1]] = grads_send[z_hi, n]
-    for batch in range(2):
+    for batch in range(len(BATCHES)):
         for i in range(7):
             grads_copy(batch, i, ring[i], grads_place(*ring[i]), ring_ids[i]).wait_recv()
     grads_wide[...] = grads_recv[...].reshape(1024, 128).astype(f32)
@@ -323,12 +336,13 @@
         pair_copy(chunk).wait_send()
         for owner_hi in range(2):
             reduce_copy(chunk, owner_hi, 0).wait_send()
-    for batch in range(2):
+    for batch in range(len(BATCHES)):
         for i in range(7):
             grads_copy(batch, i, ring[i], own_grads, ring_ids[i]).wait_send()
-    for i in range(15):
-        a_send(i, here, sibling).wait_send()
-        b_send(i, here, sibling).wait_send()
+    for way in range(2):
+        for i in range(19):
+            half = i >= 3 and i % 4 in (1, 2)
+            query_copy(way, (x, y), pl.ds(0, 1024) if half else every, i, at(way, 1, 0)).wait_send()
     for i in range(7):
         square_copy(i, own_place, ring_ids[i]).wait_send()
 
@@ -363,7 +377,7 @@
     hbm = pl.BlockSpec(memory_space=pltpu.HBM)
     return pl.pallas_call(
         kernel,
-        out_shape=jax.ShapeDtypeStruct((32, 2048), f32),
+        out_shape=pltpu.VMEM((32, 2048), f32),
         in_specs=[hbm] * 6,
         out_specs=vmem,
         scratch_shapes=[
@@ -398,28 +412,31 @@
             dma((8,)),
             dma((16,)),
             dma((16,)),
-            dma((14,)),
-            dma((16,)),
+            dma((7 * len(BATCHES),)),
+            dma((8 * len(BATCHES),)),
             dma((3,)),
-            dma((15,)),
-            dma((16,)),
-            dma((15,)),
-            dma((16,)),
+            dma((38,)),
+            dma((32,)),
             dma((7,)),
             dma((8,)),
             dma((7,)),
             dma((8,)),
         ],
         compiler_params=pltpu.CompilerParams(
-            collective_id=0, has_side_effects=True, vmem_limit_bytes=64 * 2**20 - 512 * 1024
+            collective_id=0, has_side_effects=True, vmem_limit_bytes=50 * 2**20
         ),
     )(
-        lengths,
-        out_grads.reshape(8, 512, 2048),
-        activations.reshape(8, 512, 512),
-        proj_in.T,
-        proj_out.T,
-        query_grads,
+        *(
+            pltpu.with_memory_space_constraint(array, pltpu.HBM)
+            for array in (
+                lengths,
+                out_grads.reshape(8, 512, 2048),
+                activations.reshape(8, 512, 512),
+                proj_in.T,
+                proj_out.T,
+                query_grads,
+            )
+        )
     )
 
 

time: 38.7 us -> 35.6 us (0.920)
  Pallas kernels: 36.9 us -> 34.7 us
  local copies, waits for them, and re-layouts: 1.67 us -> 0.71 us
    pallas_call x1, Pallas kernels: 36.9 us -> 34.7 us  [on_device(): pl.pallas_call(kernel, out_shape=pltpu.VMEM((32, 2048), f32), in_specs=[h...]
    unnamed x1, local copies, waits for them, and re-layouts: 1.67 us -> 0.71 us
where the time goes in v2:
time: 35.6 us; the launch traced here: 35.4 us
  Pallas kernels  34.7 us (97%)
  local copies, waits for them, and re-layouts  0.71 us (2%)
    pallas_call x1, Pallas kernels, on_device(): pl.pallas_call(kernel, out_shape=pltpu.VMEM((32, 2048), f32), in_specs=[h...  34.7 us

profile of v2, /device:TPU:1, one launch (start us, length us, event | category | flops | bytes accessed | tf_op | source)
XLA Modules:
  0.0 35.4 jit_solution(16908160161317677090)
XLA Ops:
  0.0 34.7 %shard_map.64 = f32[32,2048]{1,0:T(8,128)S(1)} custom-call(s32[32]{0:T(128)} %lengths_in.1, bf16[8,512,2048]{2,1,0:T(8,128)(2,1)} %bitcast.4, bf16[8,512,512]{2,1,0:T(8,128)(2,1)} %bitcast.5, bf16[64,512]{1,0:T(8,128)(2,1)} %bitcast.7, bf16[64,2048]{1,0:T(8,128)(2,1)} %bitcast.6, bf16[64,1024]{1,0:T(8,128)(2,1)} %queries_in.1), custom_call_target="tpu_custom_call" | custom-call | tf_op jit(solution)/shard_map/pallas_call | solution.py:378
  34.7 0.7 %copy.8 = f32[32,2048]{1,0:T(8,128)} copy(f32[32,2048]{1,0:T(8,128)S(1)} %shard_map.64) | data formatting | bytes 524288

commit v3 on v2

--- a/solution.py
+++ b/solution.py
@@ -16,9 +16,9 @@
 CHUNKS = 8
 AHEAD = 3
 REDUCE_LAG = 2
-QUERY_STEPS = (1, 5, 8, 10, 12)
+QUERY_STEPS = (1,5,8,10,12)
 BATCHES = ((0, 4), (4, 7), (7, 8))
-LAG = 7
+LAG = 8
 RING = ((2, 0), (2, 1), (1, 0), (1, 1), (3, 0), (3, 1), (0, 1))
 
 
@@ -29,7 +29,7 @@
 def kernel(
     lengths_in, out_grads, activations, proj_in_in, proj_out_in, queries_in,
     scores,
-    lengths, query_grads, proj_in_t, proj_out_t, out_held, act_held, w_out, w_in,
+    lengths, query_grads, proj_in_t, proj_out_t, held_rows, weights,
     own_part, pair_send, pair_recv, reduce_send, reduce_recv,
     grads_send, grads_recv, grads_wide, train,
     queries, square_part, square_send, square_recv,
@@ -80,10 +80,10 @@
             rows = pl.ds(pl.multiple_of((core + half) % 2 * 256, 256), 256)
             held = pl.ds(half * 256, 256)
             yield pltpu.make_async_copy(
-                out_grads.at[chunk, rows], out_held.at[chunk, held], load_sem.at[chunk * 4 + half]
+                out_grads.at[chunk, rows], held_rows.at[chunk, held, pl.ds(0, 2048)], load_sem.at[chunk * 4 + half]
             )
             yield pltpu.make_async_copy(
-                activations.at[chunk, rows], act_held.at[chunk, held], load_sem.at[chunk * 4 + 2 + half]
+                activations.at[chunk, rows], held_rows.at[chunk, held, pl.ds(2048, 512)], load_sem.at[chunk * 4 + 2 + half]
             )
 
     small = [
@@ -94,7 +94,7 @@
     ]
     for load in small + list(loads(0)):
         load.start()
-    for load in small:
+    for load in small[:2]:
         load.wait()
     for chunk in range(1, AHEAD):
         for load in loads(chunk):
@@ -105,8 +105,10 @@
     place_out = (lane == (rank_row % 2) * 32 + rank_row // 2).astype(bf16)
     place_in = (lane == rank_row + 64).astype(bf16)
     columns = (((0,), (0,)), ((), ()))
-    w_in[...] = lax.dot_general(proj_in_t[...], place_in, columns, preferred_element_type=f32).astype(bf16)
-    w_out[...] = lax.dot_general(proj_out_t[...], place_out, columns, preferred_element_type=f32).astype(bf16)
+    weights[2048:2560] = lax.dot_general(proj_in_t[...], place_in, columns, preferred_element_type=f32).astype(bf16)
+    weights[0:2048] = lax.dot_general(proj_out_t[...], place_out, columns, preferred_element_type=f32).astype(bf16)
+    for load in small[2:]:
+        load.wait()
 
     half_columns = pl.ds(pl.multiple_of(core * 1024, 1024), 1024)
     swap_out = remote(
@@ -119,10 +121,6 @@
         queries.at[here, :, half_columns],
         swap_sem.at[2],
     )
-
-    pl.semaphore_wait(barrier, len(peers))
-    swap_out.start()
-    swap_own.start()
 
     def at(way, along, across):
         step_x, step_y = (along, across) if way == 0 else (across, along)
@@ -198,8 +196,7 @@
             for load in loads(chunk + AHEAD):
                 load.start()
 
-        total = dot(out_held[chunk], w_out[...])
-        total += dot(act_held[chunk], w_in[...])
+        total = dot(held_rows[chunk], weights[...])
         kept = []
         for place in range(4):
             owner = ((core + place // 2) % 2) * 2 + place % 2
@@ -209,6 +206,13 @@
         own_part[chunk, 128:256] = kept[1]
         pair_send[chunk, 0:128] = kept[2]
         pair_send[chunk, 128:256] = kept[3]
+
+        @pl.when(chunk == 0)
+        def _():
+            pl.semaphore_wait(barrier, len(peers))
+            swap_out.start()
+            swap_own.start()
+
         pair_copy(chunk).start()
     def reduce(chunk):
         pair_copy(chunk).wait_recv()
@@ -277,20 +281,29 @@
         for column in range(4):
             spread[source * 128 + column * 32 : source * 128 + column * 32 + 32, column * 128 : column * 128 + 128] = pattern
 
+
+    own_place = part_place(z, core)
+
+    def square_rows(way, across):
+        def one(along, carry):
+            owner_x, owner_y = at(way, along, across)
+            owner = owner_x * SIDE + owner_y
+            wide = queries[owner, way * 16 : way * 16 + 16].astype(f32)
+            squares = wide * wide
+            total = squares[:, 0:128]
+            for column in range(1, 16):
+                total += squares[:, column * 128 : column * 128 + 128]
+            square_part[pl.ds(pl.multiple_of(owner * 32 + way * 16, 16), 16)] = total
+            return carry
+
+        lax.fori_loop(0, SIDE, one, 0)
+
+    for way in range(2):
+        for across in (0, 1, 3):
+            square_rows(way, across)
     opposite_second()
-
-    own_place = part_place(z, core)
-
-    def square_rows(block, carry):
-        wide = queries[block].astype(f32)
-        squares = wide * wide
-        total = squares[:, 0:128]
-        for column in range(1, 16):
-            total += squares[:, column * 128 : column * 128 + 128]
-        square_part[pl.ds(pl.multiple_of(block * 32, 32), 32)] = total
-        return carry
-
-    lax.fori_loop(0, 16, square_rows, 0)
+    for way in range(2):
+        square_rows(way, 2)
     sums = lax.dot_general(
         jnp.ones((8, 128), f32), square_part[...], (((1,), (1,)), ((), ())),
         precision=lax.Precision.HIGHEST, preferred_element_type=f32,
@@ -318,19 +331,21 @@
     for j in range(16):
         train[:, j * 128 : j * 128 + 128] = grads_wide[pl.ds(j, 64, stride=16), :].astype(bf16)
 
-    products = lax.dot_general(
-        train[...], queries[...].reshape(512, 2048), (((1,), (1,)), ((), ())), preferred_element_type=f32
-    )
-    part_send[...] = products.astype(bf16).reshape(2, 32, 512)
-
-    def part_copy(index, peer, place, to):
+    def part_copy(half, index, peer, place, to):
         return remote(
-            part_send.at[peer[0] % 2], part_recv.at[place], part_ssem.at[index], part_rsem.at[place], to
-        )
-
-    for i in range(7):
-        part_copy(i, ring[i], own_place, ring_ids[i]).start()
-    part_recv[own_place] = part_send[z_lo]
+            part_send.at[half, peer[0] % 2], part_recv.at[half, place],
+            part_ssem.at[half * 7 + index], part_rsem.at[half * 8 + place], to,
+        )
+
+    for half in range(2):
+        products = lax.dot_general(
+            train[...], queries[half * 8 : half * 8 + 8].reshape(256, 2048), (((1,), (1,)), ((), ())),
+            preferred_element_type=f32,
+        )
+        part_send[half] = products.astype(bf16).reshape(2, 32, 256)
+        for i in range(7):
+            part_copy(half, i, ring[i], own_place, ring_ids[i]).start()
+        part_recv[half, own_place] = part_send[half, z_lo]
 
     for chunk in range(CHUNKS):
         pair_copy(chunk).wait_send()
@@ -357,18 +372,24 @@
     spread_squares = sum(dot(piece, spread[...]) for piece in pieces)
     scales = lax.rsqrt(spread_squares + eps)
 
+    for half in range(2):
+        for i in range(7):
+            part_copy(half, i, ring[i], part_place(*ring[i]), ring_ids[i]).wait_recv()
+        for place in range(8):
+            for group in range(2):
+                part_rows[half, group * 32 : group * 32 + 32, place * 128 : place * 128 + 128] = part_recv[
+                    half, place, :, group * 128 : group * 128 + 128
+                ]
+        result = dot(part_rows[half], spread[...])
+        for group in range(2):
+            first = half * 2 + group
+            scores[:, first * 512 : first * 512 + 512] = (
+                result[group * 32 : group * 32 + 32] * scales[first : first + 1]
+            )
+
     for i in range(7):
-        part_copy(i, ring[i], part_place(*ring[i]), ring_ids[i]).wait_recv()
-    for place in range(8):
-        for group in range(4):
-            part_rows[group * 32 : group * 32 + 32, place * 128 : place * 128 + 128] = part_recv[
-                place, :, group * 128 : group * 128 + 128
-            ]
-    result = dot(part_rows[...], spread[...])
-    for group in range(4):
-        scores[:, group * 512 : group * 512 + 512] = result[group * 32 : group * 32 + 32] * scales[group : group + 1]
-    for i in range(7):
-        part_copy(i, ring[i], own_place, ring_ids[i]).wait_send()
+        for half in range(2):
+            part_copy(half, i, ring[i], own_place, ring_ids[i]).wait_send()
 
 
 def on_device(activations, out_grads, lengths, proj_in, proj_out, query_grads):
@@ -385,10 +406,8 @@
             pltpu.VMEM((64, 1024), bf16),
             pltpu.VMEM((64, 512), bf16),
             pltpu.VMEM((64, 2048), bf16),
-            pltpu.VMEM((8, 512, 2048), bf16),
-            pltpu.VMEM((8, 512, 512), bf16),
-            pltpu.VMEM((2048, 128), bf16),
-            pltpu.VMEM((512, 128), bf16),
+            pltpu.VMEM((8, 512, 2560), bf16),
+            pltpu.VMEM((2560, 128), bf16),
             pltpu.VMEM((8, 256, 128), f32),
             pltpu.VMEM((8, 256, 128), f32),
             pltpu.VMEM((8, 256, 128), f32),
@@ -402,9 +421,9 @@
             pltpu.VMEM((512, 128), f32),
             pltpu.VMEM((8, 128), f32),
             pltpu.VMEM((8, 8, 128), f32),
-            pltpu.VMEM((2, 32, 512), bf16),
-            pltpu.VMEM((8, 32, 512), bf16),
-            pltpu.VMEM((128, 1024), bf16),
+            pltpu.VMEM((2, 2, 32, 256), bf16),
+            pltpu.VMEM((2, 8, 32, 256), bf16),
+            pltpu.VMEM((2, 64, 1024), bf16),
             pltpu.VMEM((1024, 512), bf16),
             dma((4,)),
             dma((32,)),
@@ -419,8 +438,8 @@
             dma((32,)),
             dma((7,)),
             dma((8,)),
-            dma((7,)),
-            dma((8,)),
+            dma((14,)),
+            dma((16,)),
         ],
         compiler_params=pltpu.CompilerParams(
             collective_id=0, has_side_effects=True, vmem_limit_bytes=50 * 2**20

time: 35.6 us -> 34.6 us (0.972)
  Pallas kernels: 34.7 us -> 33.7 us
    pallas_call x1, Pallas kernels: 34.7 us -> 33.7 us  [on_device(): pl.pallas_call(kernel, out_shape=pltpu.VMEM((32, 2048), f32), in_specs=[h...]
where the time goes in v3:
time: 34.6 us; the launch traced here: 34.5 us
  Pallas kernels  33.7 us (97%)
  local copies, waits for them, and re-layouts  0.71 us (2%)
    pallas_call x1, Pallas kernels, on_device(): pl.pallas_call(kernel, out_shape=pltpu.VMEM((32, 2048), f32), in_specs=[h...  33.7 us
    unnamed x1, local copies, waits for them, and re-layouts  0.71 us

profile of v3, /device:TPU:1, one launch (start us, length us, event | category | flops | bytes accessed | tf_op | source)
XLA Modules:
  0.0 34.5 jit_solution(4845845998023699063)
XLA Ops:
  0.0 33.7 %shard_map.64 = f32[32,2048]{1,0:T(8,128)S(1)} custom-call(s32[32]{0:T(128)} %lengths_in.1, bf16[8,512,2048]{2,1,0:T(8,128)(2,1)} %bitcast.4, bf16[8,512,512]{2,1,0:T(8,128)(2,1)} %bitcast.5, bf16[64,512]{1,0:T(8,128)(2,1)} %bitcast.7, bf16[64,2048]{1,0:T(8,128)(2,1)} %bitcast.6, bf16[64,1024]{1,0:T(8,128)(2,1)} %queries_in.1), custom_call_target="tpu_custom_call" | custom-call | tf_op jit(solution)/shard_map/pallas_call | solution.py:399
  33.8 0.7 %copy.8 = f32[32,2048]{1,0:T(8,128)} copy(f32[32,2048]{1,0:T(8,128)S(1)} %shard_map.64) | data formatting | bytes 524288

commit v4 on v3

--- a/solution.py
+++ b/solution.py
@@ -327,7 +327,10 @@
     for batch in range(len(BATCHES)):
         for i in range(7):
             grads_copy(batch, i, ring[i], grads_place(*ring[i]), ring_ids[i]).wait_recv()
-    grads_wide[...] = grads_recv[...].reshape(1024, 128).astype(f32)
+        first, last = BATCHES[batch]
+        for block in range(2):
+            rows = slice(block * 512 + first * 64, block * 512 + last * 64)
+            grads_wide[rows] = grads_recv[block, first:last].reshape((last - first) * 64, 128).astype(f32)
     for j in range(16):
         train[:, j * 128 : j * 128 + 128] = grads_wide[pl.ds(j, 64, stride=16), :].astype(bf16)
 

time: 34.6 us -> 34.6 us (level)
  no operation moved by 1% of the time
where the time goes in v4:
time: 34.6 us; the launch traced here: 34.4 us
  Pallas kernels  33.7 us (97%)
  local copies, waits for them, and re-layouts  0.71 us (2%)
    pallas_call x1, Pallas kernels, on_device(): pl.pallas_call(kernel, out_shape=pltpu.VMEM((32, 2048), f32), in_specs=[h...  33.7 us
    unnamed x1, local copies, waits for them, and re-layouts  0.71 us

profile of v4, /device:TPU:1, one launch (start us, length us, event | category | flops | bytes accessed | tf_op | source)
XLA Modules:
  0.0 34.4 jit_solution(405750631766374506)
XLA Ops:
  0.0 33.7 %shard_map.64 = f32[32,2048]{1,0:T(8,128)S(1)} custom-call(s32[32]{0:T(128)} %lengths_in.1, bf16[8,512,2048]{2,1,0:T(8,128)(2,1)} %bitcast.4, bf16[8,512,512]{2,1,0:T(8,128)(2,1)} %bitcast.5, bf16[64,512]{1,0:T(8,128)(2,1)} %bitcast.7, bf16[64,2048]{1,0:T(8,128)(2,1)} %bitcast.6, bf16[64,1024]{1,0:T(8,128)(2,1)} %queries_in.1), custom_call_target="tpu_custom_call" | custom-call | tf_op jit(solution)/shard_map/pallas_call | solution.py:402
  33.7 0.7 %copy.8 = f32[32,2048]{1,0:T(8,128)} copy(f32[32,2048]{1,0:T(8,128)S(1)} %shard_map.64) | data formatting | bytes 524288
